TPU v7x, 128 devices: a whole 4x4x4 slice. The times are simulated.
128 devices in a mesh: lat: 8 (over y_hi, x), lon: 16 (over z, y_lo, core).
Axes of the slice: x: 4, y: 4 (y_hi: 2, y_lo: 2; y = y_hi * 2 + y_lo), z: 4, core: 2. Of those that a mesh axis runs over, the one named last changes fastest.
Arguments:
- station_tile: int32 [65536, 1], P(('lat', 'lon')), may hold values from 0 to 127; in each aligned block of 512 rows (0 to 511, 512 to 1023, ...) at most 8 rows name the same one
- station_cell: int32 [65536], P(('lat', 'lon')), may hold values from 0 to 8191
- station_offset: float32 [2, 65536], P(None, ('lat', 'lon')), may hold values from -0.5 to 0.5
- station_values: float32 [4, 65536], P(None, ('lat', 'lon')), may hold values from -6 to 6
- covariates: bfloat16 [8, 512, 2048], P(None, 'lat', 'lon'), may hold values from -6 to 6
- target_tile: int32 [32768, 1], P(('lat', 'lon')), may hold values from 0 to 127; in each aligned block of 256 rows (0 to 255, 256 to 511, ...) at most 4 rows name the same one
- target_cell: int32 [32768], P(('lat', 'lon')), may hold values from 0 to 8191
- target_offset: float32 [2, 32768], P(None, ('lat', 'lon')), may hold values from -0.5 to 0.5
- lift_weight: bfloat16 [13, 64], replicated, may hold values from -1.75 to 1.75
- first_kernel: bfloat16 [64, 1600], replicated, may hold values from -0.15625 to 0.15625
- second_kernel: bfloat16 [64, 1600], replicated, may hold values from -0.15625 to 0.15625
- out_weight: float32 [64, 2], replicated, may hold values from -0.75 to 0.75
- cotangent: float32 [2, 32768], P(None, ('lat', 'lon')), may hold values from -0.046875 to 0.046875
Outputs:
- predictions: float32 [2, 32768], P(None, ('lat', 'lon'))
- grad_lift: float32 [13, 64], replicated
- grad_first: float32 [64, 1600], replicated
- grad_second: float32 [64, 1600], replicated
- grad_out: float32 [64, 2], replicated
Inputs may be any that keep to these rules, and one draw needn't show every extreme that they name: `station_tile`: tiles are numbered band * 16 + column tile. Among the rows of one device no tile is named more than 8 times. `target_tile`: tiles are numbered as for stations. Among the rows of one device no tile is named more than 4 times.
All inputs are finite; a program needn't handle non-finite values.
Results may differ from a plain program's by a relative error of at most 0.0034.
The roundings to bfloat16 on the way count: a program that leaves them out, or rounds other values in their place, can miss the bound.
Values may be sent and summed in bfloat16 or wider, within the bound.
No kernel may reach another device: no remote copies, remote signals or barrier semaphores. Data moves between devices by JAX's collectives and lax.ppermute only.
A program may use at most 320 MiB of HBM per device.

v0:
```python
import jax
import jax.numpy as jnp
import numpy as np
from jax import lax
from jax.experimental import pallas as pl
from jax.experimental.pallas import tpu as pltpu
from jax.sharding import PartitionSpec as P

KERNEL = 5
REACH = 4
INV = 1.0 / 4.5
F32 = jnp.float32
BF16 = jnp.bfloat16
BANDS = 8
LONS = 16
TILES = 128
SIDES = (3, 4)
ENDS = (1, 6)
CORNERS = (0, 2, 5, 7)
OFFS = ((-1, -1), (-1, 0), (-1, 1), (0, -1), (0, 1), (1, -1), (1, 0), (1, 1), (0, 0))
NT = (((1,), (1,)), ((), ()))
NN = (((1,), (0,)), ((), ()))
SIX = ((0, 0), (0, 1), (1, 0), (1, 1), (0, 2), (2, 0))


def dot(a, b, dims=NN):
    return lax.dot_general(a, b, dims, preferred_element_type=F32)


def iota(shape, axis):
    return lax.broadcasted_iota(jnp.int32, shape, axis)


def split2(x):
    hi = x.astype(BF16)
    return hi, (x - hi.astype(F32)).astype(BF16)


def split3(x):
    hi = x.astype(BF16)
    rest = x - hi.astype(F32)
    mid = rest.astype(BF16)
    return hi, mid, (rest - mid.astype(F32)).astype(BF16)


def rounded(x):
    return x.astype(BF16).astype(F32)


def as_bf16(mask):
    return mask.astype(F32).astype(BF16)


def reaches(cell, di, dj, reach):
    row, col = cell >> 7, cell & 127
    near = row >= 0
    if di == -1:
        near = near & (row >= 64 - reach)
    if di == 1:
        near = near & (row < reach)
    if dj == -1:
        near = near & (col >= 128 - reach)
    if dj == 1:
        near = near & (col < reach)
    return near


def ranked(dests):
    count = dests[0].shape[1]
    earlier = as_bf16(iota((count, count), 0) < iota((count, count), 1))
    hits = [iota((TILES, count), 0) == dest for dest in dests]
    hits_b = [as_bf16(h) for h in hits]
    before = dot(jnp.concatenate(hits_b, axis=0), earlier)
    ranks = []
    for i, h in enumerate(hits):
        mine = before[TILES * i : TILES * i + TILES]
        ranks.append(jnp.sum(jnp.where(h, mine, 0.0), axis=0, keepdims=True))
    return hits_b, ranks


def pack_kernel(
    st_tile,
    st_cell,
    st_off,
    st_val,
    tg_tile,
    tg_cell,
    tg_off,
    tg_cot,
    cov,
    send,
    tg_rank,
    to_east,
    to_west,
):
    n_s, n_t = st_tile.shape[1], tg_tile.shape[1]
    s_cell, t_cell = st_cell[...], tg_cell[...]
    s_tile, t_tile = st_tile[...], tg_tile[...]
    s_rec = jnp.concatenate(
        [jnp.ones((1, n_s), F32), st_val[...], s_cell.astype(F32), st_off[...]], axis=0
    )
    t_rec = jnp.concatenate(
        [
            tg_cot[...],
            t_cell.astype(F32),
            tg_off[...],
            jnp.ones((1, n_t), F32),
            jnp.zeros((2, n_t), F32),
        ],
        axis=0,
    )
    s_dests, t_dests = [], []
    for dests, tile, cell, reach in ((s_dests, s_tile, s_cell, 8), (t_dests, t_tile, t_cell, 6)):
        for di, dj in OFFS[:8]:
            to = ((tile >> 4) - di) * LONS + (((tile & 15) - dj) & 15)
            dests.append(jnp.where(reaches(cell, di, dj, reach), to, -1))
        dests.append(tile)
    s_hits, s_ranks = ranked(s_dests)
    t_hits, t_ranks = ranked(t_dests)
    lane = iota((TILES, TILES), 1)

    def slots(r):
        s_rows = [jnp.where(s_ranks[r] == k, s_rec, 0.0) for k in range(8)]
        hi, mid, rest = split3(jnp.concatenate(s_rows, axis=0))
        s_found = dot(s_hits[r], jnp.concatenate([hi, rest, mid], axis=0), NT)
        first = s_found[:, 0:128]
        second = jnp.concatenate([s_found[:, 128:192], jnp.zeros((TILES, 64), F32)], axis=1)
        s_found = first + second + pltpu.roll(first, 64, 1)
        t_rows = [jnp.where(t_ranks[r] == k, t_rec, 0.0) for k in range(4)]
        hi, mid, rest = split3(jnp.concatenate(t_rows, axis=0))
        blank = jnp.zeros((64, n_t), BF16)
        tail = jnp.zeros((32, n_t), BF16)
        parts = jnp.concatenate([blank, hi, rest, blank, mid, tail], axis=0)
        t_found = dot(t_hits[r], parts, NT)
        first = t_found[:, 0:128]
        t_found = first + t_found[:, 128:256] + pltpu.roll(first, 96, 1)
        return jnp.where(lane < 64, s_found, jnp.where(lane < 96, t_found, 0.0))

    parts = split3(slots(8))
    tg_rank[8:16, :] = jnp.broadcast_to(t_ranks[8], (8, n_t))
    dest = iota((TILES, TILES), 0)
    for r in range(8):
        tg_rank[r : r + 1, :] = jnp.where(t_dests[r] < 0, -1.0, t_ranks[r])
        own = (lane >= 96) & (lane < 104) & (dest == lane - 96 + 8 * r)
        if r < 4:
            own = own | ((lane >= 104) & (lane < 112) & (dest == lane - 104 + 64 + 8 * r))
        pick = as_bf16(own)
        send[:, r, :] = slots(r) + sum(dot(part, pick) for part in parts)

    blank = jnp.zeros((64, 128), F32)
    east, west = [], []
    for v in range(8):
        turned = jnp.concatenate([cov[v].astype(F32), blank], axis=0).T
        east.append(turned[120:128])
        west.append(turned[0:8])
    to_east[...] = jnp.concatenate(east, axis=0).astype(BF16)
    to_west[...] = jnp.concatenate(west, axis=0).astype(BF16)

    band, lon = lax.axis_index("lat"), lax.axis_index("lon")
    lane = iota((8, 128), 1)
    for r in CORNERS:
        di, dj = OFFS[r]
        rows = cov[:, 48:64, :] if di < 0 else cov[:, 0:16, :]
        rows = rows.astype(F32)
        block = jnp.zeros((8, 128), F32)
        for i in range(4):
            line = rows[:, 12 + i if di < 0 else i, :]
            to = 112 + 4 * i
            line = pltpu.roll(line, (to - (124 if dj < 0 else 0)) % 128, 1)
            block = jnp.where((lane >= to) & (lane < to + 4), line, block)
        to_band = band - di

        @pl.when((to_band >= 0) & (to_band < BANDS))
        def _(block=block, to_band=to_band, dj=dj):
            dest = to_band * LONS + ((lon - dj) & 15)
            send[pl.ds(dest, 1)] += block[None]


def build_weights(k1, k2, lift_w, out_w, t1, t2, t3, wbig, wg, wdec, kt):
    half = jnp.zeros((128, 64), F32)
    for b in range(13):
        wide = 128 if b < 12 else 64
        piece = jnp.concatenate(
            [k1[:, 128 * b : 128 * b + wide], k2[:, 128 * b : 128 * b + wide]], axis=0
        ).astype(F32)
        if wide == 64:
            piece = jnp.concatenate([piece, half], axis=1)
        kt[128 * b : 128 * b + 128, :] = piece.T
    low = iota((64, 128), 1) < 64
    none = jnp.zeros((64, 128), F32)
    for q in range(KERNEL):
        v = [kt[pl.ds(p * 5 + q, 64, stride=25), :] for p in range(5)]
        turned = [pltpu.roll(x, 64, 1) for x in v]
        for w in range(8):
            rows = slice(64 * w, 64 * w + 64)
            for side, p in enumerate((w, w - 2)):
                lanes = slice(128 * side, 128 * side + 128)
                if p < 0 or p > 5:
                    g1 = g2 = g3 = none
                else:
                    here, before = (v[p], turned[p]) if p < 5 else (none, none), (
                        (v[p - 1], turned[p - 1]) if p > 0 else (none, none)
                    )
                    g1 = jnp.where(low, here[0], before[1])
                    g2 = jnp.where(low, here[1], before[0])
                    pair = jnp.concatenate(
                        [v[4 - p] if p < 5 else none, v[5 - p] if p > 0 else none], axis=0
                    )
                    g3 = pair.T[64:128]
                t1[q, rows, lanes] = g1.astype(BF16)
                t2[q, rows, lanes] = g2.astype(BF16)
                t3[4 - q, rows, lanes] = g3.astype(BF16)
    same = (iota((8, 512), 1) >> 6) == iota((8, 512), 0)
    lift2 = lift_w[...].astype(F32)
    lift2 = jnp.concatenate([lift2, lift2], axis=1)
    rows = []
    for k in range(13):
        row = jnp.concatenate([lift2[k : k + 1, :]] * 4, axis=1)
        rows.append(jnp.where(same, row, 0.0))
    rows += [jnp.zeros((8, 512), F32)] * 3
    wbig[...] = jnp.concatenate(rows, axis=0).astype(BF16)
    out2 = jnp.concatenate([out_w[...], out_w[...]], axis=1)
    parts = [x.astype(F32) for x in split3(out2)]
    blank = jnp.zeros((16, 512), F32)
    rows = []
    for x in parts:
        two = [jnp.concatenate([x[v : v + 1, :]] * 4, axis=1) for v in range(2)]
        rows.append(jnp.concatenate([jnp.where(same, y, 0.0) for y in two], axis=0))
    stack = [rows[0], rows[1], rows[2], rows[0], rows[1], rows[0], blank, blank]
    wg[...] = jnp.concatenate(stack, axis=0).astype(BF16)
    sub = iota((8, 256), 0)
    same = (iota((8, 256), 1) >> 6) == (sub & 3)
    rows = []
    for x in parts:
        two = [jnp.concatenate([x[v : v + 1, :]] * 2, axis=1) for v in range(2)]
        rows.append(jnp.where(same, jnp.where(sub < 4, two[0], two[1]), 0.0))
    wdec[...] = jnp.concatenate(rows + [jnp.zeros((8, 256), F32)], axis=0).astype(BF16)


def centre(cell, row_shift, col_shift):
    row = jnp.floor(cell * (1.0 / 128.0))
    col = cell - row * 128.0
    return row + row_shift, col + col_shift


def factor(place, centre_row, offset_row):
    gap = place - centre_row
    distance = gap - offset_row
    return jnp.where(jnp.abs(gap) <= float(REACH), jnp.exp(-(distance * distance) * INV), 0.0)


def places(count, start):
    return (iota((count, 128), 0) + start).astype(F32)


def repeated(start):
    return ((iota((128, 128), 0) & 15) + start).astype(F32)


def conv_rows(x_ref, t_ref, first, count, length):
    total = None
    for q in range(KERNEL):
        before = x_ref[q, pl.ds(first - 1, count), 0:length, 128:256]
        here = x_ref[q, pl.ds(first, count), 0:length, :]
        after = x_ref[q, pl.ds(first + 1, count), 0:length, 0:128]
        lhs = jnp.concatenate([before, here, after], axis=2).reshape(count * length, 512)
        part = dot(lhs, t_ref[q])
        total = part if total is None else total + part
    return total


def windows(x_ref, q, first):
    before = x_ref[q, first - 1 : first + 15, 0:128, 128:256]
    here = x_ref[q, first : first + 16, 0:128, :]
    after = x_ref[q, first + 1 : first + 17, 0:128, 0:128]
    return jnp.concatenate([before, here, after], axis=2).reshape(2048, 512)


def shifted(x, by):
    return x if by == 0 else pltpu.roll(x, x.shape[0] - by, 0)


def fold_rows(corr, q):
    even = corr[0:64, 0:384] + corr[128:192, 128:512]
    odd = corr[64:128, 0:384] + corr[192:256, 128:512]
    if q % 2 == 0:
        return even + pltpu.roll(odd, 384 - 64, 1)
    return pltpu.roll(even, 64, 1) + odd


def kernel_grad_rows(gt, x_ref, base, first):
    lines = [
        fold_rows(dot(gt[...], windows(x_ref, base + q, first)), q) for q in range(KERNEL)
    ]
    lane = iota((64, 128), 1)
    low = lane < 64
    tiles = [lines[0][:, 0:128], lines[0][:, 128:256]]
    tiles.append(jnp.where(low, lines[0][:, 256:384], lines[1][:, 0:128]))
    tiles += [lines[1][:, 128:256], lines[1][:, 256:384]]
    tiles += [lines[2][:, 0:128], lines[2][:, 128:256]]
    tiles.append(jnp.where(low, lines[2][:, 256:384], lines[3][:, 0:128]))
    tiles += [lines[3][:, 128:256], lines[3][:, 256:384]]
    tiles += [lines[4][:, 0:128], lines[4][:, 128:256]]
    tiles += [jnp.where(low, lines[4][:, 256:384], 0.0), jnp.zeros((64, 128), F32)]
    quarter = (lane & 63) < 32
    rows = []
    for r in range(7):
        a, b = tiles[2 * r], tiles[2 * r + 1]
        rows.append(
            (
                jnp.where(quarter, a, pltpu.roll(b, 32, 1)),
                jnp.where(quarter, pltpu.roll(a, 96, 1), b),
            )
        )
    return rows


def neighbour_count(tr, start, stride_rows, slots):
    most = tr[0, pl.ds(start, slots, stride=8), :]
    for r in range(1, 8):
        most = jnp.maximum(most, tr[r, pl.ds(start, slots, stride=8), :])
    most = jnp.max(most, axis=1, keepdims=True)
    return jnp.sum(most).astype(jnp.int32)


def spans(r):
    di, dj = OFFS[r]
    n0, n = {0: (0, 80), -1: (0, 16), 1: (64, 16)}[di]
    m0, m = {0: (0, 144), -1: (0, 16), 1: (128, 16)}[dj]
    return di, dj, n0, n, m0, m


def inside_tile(shape, row, col):
    return (row >= 0) & (row < 64) & (col >= 0) & (col < 128)


def main_kernel(
    recv,
    cov,
    north,
    south,
    west,
    east,
    k1,
    k2,
    lift_w,
    out_w,
    sel,
    out,
    tr,
    dens,
    stot,
    gt1,
    lhs_s,
    rhs_s,
    side_p,
    end_p,
    corner_p,
    side_s,
    end_s,
    corner_s,
    lgacc,
    covx,
    st_t,
    x1,
    x2,
    x3,
    win,
    lat,
    lmat,
    gt2,
    predm,
    last,
    t1,
    t2,
    t3,
    wbig,
    wg,
    wdec,
    kt,
):
    band, lon = lax.axis_index("lat"), lax.axis_index("lon")
    build_weights(k1, k2, lift_w, out_w, t1, t2, t3, wbig, wg, wdec, kt)

    for r in range(8):
        tr[r] = recv[:, r, :].T
    station_most = neighbour_count(tr, 0, 8, 8)
    target_most = neighbour_count(tr, 69, 8, 4)

    def station_step(k, carry):
        rec = tr[k, 96:104, :]
        row, col = centre(rec[5:6], REACH, REACH)
        down = factor(places(80, 0), row, rec[6:7])
        across = factor(places(144, 0), col, rec[7:8])
        for p, part in enumerate(split3(across)):
            at = pl.ds(pl.multiple_of(k * 128 + 1024 * p, 128), 128)
            rhs_s[0:144, at] = part
        for v in range(5):
            for p, part in enumerate(split3(down * rec[v : v + 1])):
                at = pl.ds(pl.multiple_of(k * 128 + 1024 * p, 128), 128)
                lhs_s[v * 80 : v * 80 + 80, at] = part
        return carry

    lax.fori_loop(0, 8, station_step, 0)
    part = None
    for a, b in SIX:
        one = dot(
            lhs_s[0:400, 1024 * a : 1024 * a + 1024], rhs_s[0:144, 1024 * b : 1024 * b + 1024], NT
        )
        part = one if part is None else part + one
    inside = inside_tile((80, 144), iota((80, 144), 0) - REACH, iota((80, 144), 1) - REACH)
    dens[...] = jnp.zeros(dens.shape, F32)
    for v in range(5):
        piece = part[v * 80 : v * 80 + 80]
        dens[v, :, 0:144] = jnp.where(inside, piece, rounded(piece))

    side_p[...] = jnp.zeros(side_p.shape, F32)
    end_p[...] = jnp.zeros(end_p.shape, F32)
    corner_p[...] = jnp.zeros(corner_p.shape, F32)

    def neighbour_station_step(k, carry):
        for r in range(8):
            di, dj, n0, n, m0, m = spans(r)
            rec = tr[r, pl.ds(pl.multiple_of(k * 8, 8), 8), :]
            row, col = centre(rec[5:6], 64.0 * di + REACH, 128.0 * dj + REACH)
            down = factor(places(n, n0), row, rec[6:7])
            across = split3(factor(places(m, m0), col, rec[7:8]))
            left = split3(jnp.concatenate([down * rec[v : v + 1] for v in range(5)], axis=0))
            left = jnp.concatenate([left[a] for a, _ in SIX], axis=1)
            right = jnp.concatenate([across[b] for _, b in SIX], axis=1)
            more = dot(left, right, NT)
            if r in SIDES:
                side_p[SIDES.index(r), :, 0:16] += more
            elif r in ENDS:
                end_p[ENDS.index(r), :, 0:144] += more
            else:
                corner_p[CORNERS.index(r), :, 0:16] += more
        return carry

    lax.fori_loop(0, station_most, neighbour_station_step, 0)
    for r in range(8):
        di, dj, n0, n, m0, m = spans(r)
        inside = inside_tile(
            (n, m),
            iota((n, m), 0) + (n0 - REACH - 64 * di),
            iota((n, m), 1) + (m0 - REACH - 128 * dj),
        )
        for v in range(5):
            if r in SIDES:
                piece = side_p[SIDES.index(r), v * n : v * n + n, 0:m]
            elif r in ENDS:
                piece = end_p[ENDS.index(r), v * n : v * n + n, 0:m]
            else:
                piece = corner_p[CORNERS.index(r), v * n : v * n + n, 0:m]
            dens[v, n0 : n0 + n, m0 : m0 + m] += jnp.where(inside, piece, rounded(piece))

    for k in range(4):
        rec = tr[k, 104:112, :]
        row, col = centre(rec[2:3], REACH, REACH)
        down = factor(places(80, 0), row, rec[3:4])
        across = factor(places(144, 0), col, rec[4:5])
        rhs_s[0:144, 128 * k : 128 * k + 128] = across.astype(BF16)
        for v in range(2):
            for p, part in enumerate(split3(down * rec[v : v + 1])):
                at = 128 * k + 512 * p
                lhs_s[v * 80 : v * 80 + 80, at : at + 128] = part
    right = rhs_s[0:144, 0:512]
    spread = sum(dot(lhs_s[0:160, 512 * p : 512 * p + 512], right, NT) for p in range(3))
    stot[...] = jnp.zeros(stot.shape, F32)
    for v in range(2):
        stot[v, :, 0:144] = spread[80 * v : 80 * v + 80]

    def gradient_rows(s8):
        hi = rounded(s8)
        mid = rounded(s8 - hi)
        rest = rounded(s8 - hi - mid)
        zero = jnp.zeros_like(s8)
        stack = jnp.concatenate([hi, hi, hi, mid, mid, rest, zero, zero], axis=0)
        return stack.T.astype(BF16)

    e_row = (iota((144, 512), 1) >> 6) - REACH
    e_col = iota((144, 512), 0) - REACH
    for block in range(9):
        rows = pl.ds(8 * block, 8)
        s8 = jnp.concatenate([stot[v, rows, :] for v in range(2)], axis=0)
        piece = dot(gradient_rows(s8)[0:144], wg[...])
        inside = inside_tile((144, 512), e_row + 8 * block, e_col)
        lgacc[block] = jnp.where(inside, piece, rounded(piece))

    side_s[...] = jnp.zeros(side_s.shape, F32)
    end_s[...] = jnp.zeros(end_s.shape, F32)
    corner_s[...] = jnp.zeros(corner_s.shape, F32)

    def neighbour_target_step(k, carry):
        for r in range(8):
            di, dj, n0, n, m0, m = spans(r)
            rec = tr[r, pl.ds(pl.multiple_of(64 + k * 8, 8), 8), :]
            row, col = centre(rec[2:3], 64.0 * di + REACH, 128.0 * dj + REACH)
            down = factor(places(n, n0), row, rec[3:4])
            across = factor(places(m, m0) if dj == 0 else repeated(m0), col, rec[4:5]).astype(BF16)
            left = jnp.concatenate([down * rec[v : v + 1] for v in range(2)], axis=0)
            left = jnp.concatenate(split3(left), axis=1)
            more = dot(left, jnp.concatenate([across] * 3, axis=1), NT)
            if r in SIDES:
                side_s[SIDES.index(r)] += more
            elif r in ENDS:
                end_s[ENDS.index(r), :, 0:144] += more
            else:
                corner_s[CORNERS.index(r)] += more
        return carry

    lax.fori_loop(0, target_most, neighbour_target_step, 0)
    for r in range(8):
        di, dj, n0, n, m0, m = spans(r)
        for v in range(2):
            if r in SIDES:
                piece = side_s[SIDES.index(r), v * n : v * n + n, 0:m]
            elif r in ENDS:
                piece = end_s[ENDS.index(r), v * n : v * n + n, 0:m]
            else:
                piece = corner_s[CORNERS.index(r), v * n : v * n + n, 0:m]
            stot[v, n0 : n0 + n, m0 : m0 + m] += piece

    def add_piece(r, block, m0, piece):
        di, dj = OFFS[r]
        kept = piece.shape[0]
        row = (iota((kept, 512), 1) >> 6) - REACH - 64 * di + 8 * block
        col = iota((kept, 512), 0) + (m0 - REACH - 128 * dj)
        piece = jnp.where(inside_tile((kept, 512), row, col), piece, rounded(piece))
        lgacc[block, m0 : m0 + kept, :] += piece

    for i, r in enumerate(ENDS):
        s8 = jnp.concatenate([end_s[i, v * 16 : v * 16 + 8, :] for v in range(2)], axis=0)
        add_piece(r, 0 if r == 1 else 8, 0, dot(gradient_rows(s8)[0:144], wg[...]))
    group = iota((8, 128), 1) >> 4
    for i, r in enumerate(SIDES):
        s8 = []
        for v in range(2):
            line = jnp.zeros((8, 128), F32)
            for block in range(8):
                at = v * 80 + 8 * block
                line = jnp.where(group == block, side_s[i, at : at + 8, :], line)
            s8.append(line)
        many = dot(gradient_rows(jnp.concatenate(s8, axis=0)), wg[...])
        m0 = 0 if r == 3 else 128
        for block in range(8):
            add_piece(r, block, m0, many[16 * block : 16 * block + 16])
    s8 = []
    for v in range(2):
        line = jnp.zeros((8, 128), F32)
        for i in range(2):
            line = jnp.where(group == i, side_s[i, v * 80 + 64 : v * 80 + 72, :], line)
        for i in range(4):
            line = jnp.where(group == 2 + i, corner_s[i, v * 16 : v * 16 + 8, :], line)
        s8.append(line)
    many = dot(gradient_rows(jnp.concatenate(s8, axis=0)), wg[...])
    for i, (r, block) in enumerate(((3, 8), (4, 8), (0, 0), (2, 0), (5, 8), (7, 8))):
        m0 = 0 if OFFS[r][1] < 0 else 128
        add_piece(r, block, m0, many[16 * i : 16 * i + 16])

    for block in range(9):
        grow = band * 64 + 8 * block - REACH + (iota((144, 512), 1) >> 6)
        grad = rounded(jnp.where((grow >= 0) & (grow < 512), lgacc[block], 0.0))
        for q in range(KERNEL):
            moved = shifted(grad, q + 2)[0:128].astype(BF16)
            x3[q, 2 * block] = moved[:, 0:256]
            x3[q, 2 * block + 1] = moved[:, 256:512]
        own = shifted(grad, REACH)[0:128]
        for side in range(2):
            i = 2 * block + side - 1
            if 0 <= i < 16:
                turned = own[:, 256 * side : 256 * side + 256].T
                gt1[:, 128 * i : 128 * i + 128] = turned.astype(BF16)

    covx[...] = jnp.zeros(covx.shape, F32)
    lane = iota((64, 128), 1)
    from_west = west[...].astype(F32).T
    from_east = east[...].astype(F32).T
    wide = jnp.zeros((64, 128), F32)
    few = jnp.zeros((4, 128), F32)
    for v in range(8):
        rows = jnp.concatenate([cov[v].astype(F32), wide], axis=1)
        rows = pltpu.roll(rows, 4, 1)
        left = pltpu.roll(
            jnp.concatenate([from_west[0:64], wide[:, 0:64]], axis=1), 124 - 8 * v, 1
        )
        right = pltpu.roll(
            jnp.concatenate([from_east[0:64], wide[:, 0:64]], axis=1), (132 - 8 * v) % 128, 1
        )
        covx[v, 4:68, 0:128] = jnp.where(lane < 4, left, rows[:, 0:128])
        right = jnp.where((lane >= 4) & (lane < 8), right, rows[:, 128:256])
        covx[v, 4:68, 128:256] = right
        for at, strip in ((0, north), (68, south)):
            rows = jnp.concatenate([strip[v].astype(F32), few], axis=1)
            covx[v, at : at + 4, :] = pltpu.roll(rows, 4, 1)
    lane = iota((8, 128), 1)
    for r in CORNERS:
        di, dj = OFFS[r]
        from_band = jnp.clip(band + di, 0, BANDS - 1)
        block = recv[from_band * LONS + ((lon + dj) & 15)]
        at, tile = (0, 0) if dj < 0 else (4, 128)
        for i in range(4):
            line = pltpu.roll(block, (at - 112 - 4 * i) % 128, 1)
            line = jnp.where((lane >= at) & (lane < at + 4), line, 0.0)
            covx[:, (0 if di < 0 else 68) + i, tile : tile + 128] += line

    x1[:, 0] = jnp.zeros((7, 144, 256), BF16)
    x1[:, 19] = jnp.zeros((7, 144, 256), BF16)

    def lift_step(block, carry):
        rows = pl.ds(pl.multiple_of(block * 8, 8), 8)
        grow = band * 64 + 8 * block - REACH + iota((8, 256), 0)
        real = (grow >= 0) & (grow < 512)
        first = dens[0, rows, :]
        below = jnp.maximum(first, 1.0)
        planes = [first] + [dens[v, rows, :] / below for v in range(1, 5)]
        planes = [rounded(x) for x in planes] + [covx[v, rows, :] for v in range(8)]
        planes = [jnp.where(real, x, 0.0) for x in planes]
        planes = planes + [jnp.zeros((8, 256), F32)] * 3
        left = jnp.concatenate(planes, axis=0).T[0:144].astype(BF16)
        st_t[block] = left
        lifted = rounded(dot(left, wbig[...]))
        for m in range(7):
            moved = shifted(lifted, m).astype(BF16)
            x1[m, 2 * block + 1] = moved[:, 0:256]
            x1[m, 2 * block + 2] = moved[:, 256:512]
        return carry

    lax.fori_loop(0, 9, lift_step, 0, unroll=9)

    def hidden_step(c, carry):
        value = jnp.maximum(conv_rows(x1, t1, 3 * c + 1, 3, 144), 0.0)
        for i in range(3):
            sr = 3 * c + i
            gone = ((sr == 0) & (band == 0)) | ((sr == 17) & (band == BANDS - 1))
            row = rounded(jnp.where(gone, 0.0, value[144 * i : 144 * i + 144]))
            for q in range(KERNEL):
                x2[q, sr] = shifted(row, q)[0:128].astype(BF16)
        return carry

    lax.fori_loop(0, 6, hidden_step, 0, unroll=6)

    for r, (upper, lower) in enumerate(kernel_grad_rows(gt1, x2, 0, 1)):
        if r == 6:
            last[0:64, :] = upper
            last[64:128, :] = lower
        else:
            lanes = slice(896 + 128 * r, 1024 + 128 * r)
            out[0:64, 0, lanes] = upper
            out[64:128, 0, lanes] = lower

    def latent_step(c, carry):
        value = conv_rows(x2, t2, 4 * c + 1, 4, 128)
        own = x1[4, pl.ds(4 * c + 2, 4), 0:128, :].reshape(512, 256)
        latent = (own.astype(F32) + value).astype(BF16)
        lat[pl.ds(4 * c, 4)] = latent.reshape(4, 128, 256)
        outs = dot(wdec[...], latent, NT)
        outs = outs[0:8] + outs[8:16] + outs[16:24]
        for i in range(4):
            lmat[pl.ds(pl.multiple_of(32 * c + 8 * i, 8), 8), :] = outs[:, 128 * i : 128 * i + 128]
        return carry

    lax.fori_loop(0, 4, latent_step, 0)

    grad_out = jnp.zeros((48, 512), F32)
    for m in range(8):
        s8 = jnp.concatenate(
            [pltpu.roll(stot[v, 4 + 8 * m : 12 + 8 * m, :], 252, 1)[:, 0:128] for v in range(2)],
            axis=0,
        )
        left = jnp.concatenate([p.astype(F32) for p in split3(s8)], axis=0).astype(BF16)
        grad_out = grad_out + dot(left, jnp.concatenate([lat[2 * m], lat[2 * m + 1]], axis=1))
    grad_out = grad_out[0:16] + grad_out[16:32] + grad_out[32:48]
    grad_out = jnp.where((iota((16, 512), 0) & 7) == (iota((16, 512), 1) >> 6), grad_out, 0.0)
    grad_out = sum(grad_out[:, 128 * i : 128 * i + 128] for i in range(4))
    grad_out = grad_out + pltpu.roll(grad_out, 64, 1)
    grad_out = jnp.concatenate(
        [jnp.sum(grad_out[8 * v : 8 * v + 8], axis=0, keepdims=True) for v in range(2)], axis=0
    )

    predm[...] = jnp.zeros(predm.shape, F32)
    n_iota = iota((128, 128), 0)
    i_row = (4 * (n_iota >> 3) + (n_iota & 3)).astype(F32)
    pieces = split3(lmat[...])
    stacked_l = jnp.concatenate(pieces, axis=1)
    pad = jnp.zeros((8, 128), F32)
    ends = []
    for lo in (0, 120):
        few = split3(jnp.concatenate([lmat[lo : lo + 8, :], pad], axis=0))
        ends.append(jnp.concatenate(few, axis=1))

    def decode_line(mixed, down, row):
        mixed = mixed * down
        eight = jnp.sum(mixed.reshape(mixed.shape[0] // 8, 8, 128), axis=0)
        lines = [jnp.sum(eight[4 * v : 4 * v + 4], axis=0, keepdims=True) for v in range(2)]
        for v in range(2):
            predm[pl.ds(row + v, 1), :] = lines[v]

    acrosses, downs = [], []
    for k in range(4):
        rec = tr[k, 104:112, :]
        row, col = centre(rec[2:3], 0.0, 0.0)
        acrosses.append(factor(places(128, 0), col, rec[4:5]).astype(BF16))
        downs.append(factor(i_row, row, rec[3:4]))
    wide = jnp.concatenate(acrosses, axis=1)
    mixed = dot(stacked_l, jnp.concatenate([wide] * 3, axis=0))
    for k in range(4):
        decode_line(mixed[:, 128 * k : 128 * k + 128], downs[k], 64 + 2 * k)

    def decode_step(k, carry):
        for r in range(8):
            di, dj = OFFS[r]
            rec = tr[r, pl.ds(pl.multiple_of(64 + k * 8, 8), 8), :]
            row, col = centre(rec[2:3], 64.0 * di, 128.0 * dj)
            across = factor(places(128, 0), col, rec[4:5]).astype(BF16)
            across = jnp.concatenate([across] * 3, axis=0)
            if di == 0:
                decode_line(dot(stacked_l, across), factor(i_row, row, rec[3:4]), 8 * r + 2 * k)
            else:
                lo = 0 if di < 0 else 120
                few = dot(ends[0 if di < 0 else 1], across)[0:8]
                decode_line(few, factor(i_row[lo : lo + 8], row, rec[3:4]), 8 * r + 2 * k)
        return carry

    lax.fori_loop(0, target_most, decode_step, 0)

    def hidden_grad_step(c, carry):
        value = conv_rows(x3, t3, 4 * c + 1, 4, 128)
        for i in range(4):
            alive = x2[2, 4 * c + i + 1].astype(F32) > 0.0
            row = rounded(jnp.where(alive, value[128 * i : 128 * i + 128], 0.0))
            gt2[:, pl.ds(pl.multiple_of(512 * c + 128 * i, 128), 128)] = row.T.astype(BF16)
        return carry

    lax.fori_loop(0, 4, hidden_grad_step, 0, unroll=4)
    for r, (upper, lower) in enumerate(kernel_grad_rows(gt2, x1, 2, 2)):
        if r == 6:
            answers = pltpu.roll(predm[...].T, 32, 1)
            upper = upper + answers[0:64]
            lower = lower + answers[64:128]
        lanes = slice(128 * r, 128 * r + 128)
        out[0:64, 0, lanes] = upper
        out[64:128, 0, lanes] = lower

    def window_step(m, carry):
        left = jnp.concatenate([st_t[m], st_t[m + 1]], axis=1)
        both = dot(left, sel[...])
        for q in range(KERNEL):
            moved = shifted(both, q + 2)[0:128].astype(BF16)
            win[2 * m, :, 128 * q : 128 * q + 128] = moved[:, 0:128]
            win[2 * m + 1, :, 128 * q : 128 * q + 128] = moved[:, 128:256]
        return carry

    lax.fori_loop(0, 8, window_step, 0, unroll=8)
    corr = dot(gt2[...], win[...].reshape(2048, 640))
    grad_lift = jnp.zeros((512, 256), F32)
    for q in range(KERNEL):
        two = jnp.concatenate(split2(corr[:, 128 * q : 128 * q + 128]), axis=1)
        grad_lift = grad_lift + dot(t1[q], two)
    grad_lift = grad_lift[:, 0:128] + grad_lift[:, 128:256]
    same = (iota((512, 128), 0) >> 6) == (iota((512, 128), 1) >> 4)
    grad_lift = jnp.where(same, grad_lift, 0.0)
    direct = dot(gt1[...], win[:, :, 256:384].reshape(2048, 128))
    same = (iota((256, 128), 0) >> 6) + 2 == (iota((256, 128), 1) >> 4)
    direct = jnp.where(same, direct, 0.0)
    total = sum(grad_lift[64 * w : 64 * w + 64] for w in range(8))
    total = total + sum(direct[64 * w : 64 * w + 64] for w in range(4))
    for by in (64, 32, 16):
        total = total + pltpu.roll(total, by, 1)
    misc = jnp.concatenate([total, grad_out, jnp.zeros((62, 128), F32)], axis=0)
    misc = jnp.where(iota((128, 128), 1) < 64, misc, 0.0)
    out[:, 0, 1664:1792] = last[...] + pltpu.roll(misc, 64, 1)


def summed_chunk(total, perm, shift):
    turned = jnp.concatenate([total, jnp.zeros((120, 128), F32)], axis=0).T
    lane = iota((32, 896), 1)
    channel = iota((32, 896), 0)
    own = (lane >= 25 * channel) & (lane < 25 * channel + 25)
    spread = jnp.zeros((32, 896), F32)
    for g in range(4):
        left = turned[32 * g : 32 * g + 32, 0:16]
        spread = spread + sum(dot(part, perm[g]) for part in split3(left))
    line = jnp.sum(jnp.where(own, spread, 0.0), axis=0, keepdims=True)
    line = jnp.broadcast_to(line, (8, 896))
    line = jnp.where(shift, pltpu.roll(line, 32, 1), line)
    return [line[0:1, 128 * t : 128 * t + 128] for t in range(7)]


def sum_kernel(recv, perm, tg_tile, tg_rank, back, pred):
    total = jnp.sum(recv[...], axis=0)
    lines = [total[:, 128 * t : 128 * t + 128] for t in range(14)]
    zero = jnp.zeros((1, 128), F32)
    shift = lax.axis_index("lat") >= BANDS // 2
    misc = jnp.where(iota((1, 128), 1) < 64, pltpu.roll(lines[13], 64, 1), 0.0)
    high = rounded(misc)
    rows = summed_chunk(jnp.concatenate(lines[0:7] + [zero], axis=0), perm, shift) + [high]
    rows += summed_chunk(jnp.concatenate(lines[7:14] + [zero], axis=0), perm, shift)
    chunk = jnp.concatenate(rows + [misc - high], axis=0).astype(BF16)
    back[...] = jnp.broadcast_to(chunk[None], back.shape)

    answers = recv[:, 0, 768:896].T
    tile = tg_tile[...]
    count = tile.shape[1]
    band, lon = tile >> 4, tile & 15
    place = iota((TILES, count), 0)
    value = [jnp.zeros((1, count), F32) for _ in range(2)]
    for r in range(9):
        di, dj = OFFS[r]
        source = (band - di) * LONS + ((lon - dj) & 15)
        pick = as_bf16(place == source)
        eight = answers[32 + 8 * r : 40 + 8 * r]
        parts = jnp.concatenate([p.astype(F32) for p in split3(eight)], axis=0)
        found = dot(parts.astype(BF16), pick)
        found = found[0:8] + found[8:16] + found[16:24]
        rank = tg_rank[r : r + 1, :]
        for v in range(2):
            for k in range(4):
                line = found[2 * k + v : 2 * k + v + 1]
                value[v] = value[v] + jnp.where(rank == float(k), line, 0.0)
    for v in range(2):
        pred[v : v + 1, :] = value[v]


def final_kernel(recv, first, second, lift, outw, wide_s):
    wide_s[...] = recv[...].astype(F32)
    low = iota((64, 128), 1) < 32
    for base, to in ((0, first), (8, second)):
        for t in range(13):
            if t < 6:
                to[:, 128 * t : 128 * t + 128] = wide_s[0:64, base + t, :]
            elif t == 6:
                to[:, 768:896] = jnp.where(
                    low, wide_s[0:64, base + 6, :], wide_s[64:128, base, :]
                )
            else:
                wide = 128 if t < 12 else 64
                to[:, 128 * t : 128 * t + wide] = wide_s[64:128, base + t - 6, 0:wide]
    turned = (wide_s[:, 7, :] + wide_s[:, 15, :]).T
    lift[...] = turned[0:13, 0:64]
    outw[...] = (wide_s[64:72, 7, 0:64] + wide_s[64:72, 15, 0:64])[0:2]


def selection():
    table = np.zeros((2, 16, 8, 2, 8, 16), np.float32)
    for group in range(2):
        for w in range(8):
            at = 4 * group + w + 2
            for k in range(16):
                table[at // 8, k, at % 8, group, w, k] = 1.0
    return table.reshape(256, 256)


def permutation():
    table = np.zeros((4, 16, 896), np.float32)
    for g in range(4):
        for r in range(7):
            at = 4 * r + (g >> 1) + 2 * (g & 1)
            if at < 25:
                q, p = at // 5, at % 5
                for c in range(32):
                    table[g, r, c * 25 + p * 5 + q] = 1.0
    return table


def ring(axis, step):
    size = lax.axis_size(axis)
    return [(i, (i + step) % size) for i in range(size)]


def shape(*dims, dtype=F32):
    return jax.ShapeDtypeStruct(dims, dtype)


def call(kernel, outs, scratch=(), limit=60):
    return pl.pallas_call(
        kernel,
        out_shape=outs,
        scratch_shapes=scratch,
        compiler_params=pltpu.CompilerParams(vmem_limit_bytes=limit * 2**20),
    )


def shards(
    station_tile,
    station_cell,
    station_offset,
    station_values,
    covariates,
    target_tile,
    target_cell,
    target_offset,
    lift_weight,
    first_kernel,
    second_kernel,
    out_weight,
    cotangent,
):
    n_s, n_t = station_cell.shape[0], target_cell.shape[0]
    axes = ("lat", "lon")
    tg_tile = target_tile.reshape(1, n_t)
    send, tg_rank, to_east, to_west = call(
        pack_kernel,
        (
            shape(TILES, 8, 128),
            shape(16, n_t),
            shape(64, 128, dtype=BF16),
            shape(64, 128, dtype=BF16),
        ),
    )(
        station_tile.reshape(1, n_s),
        station_cell.reshape(1, n_s),
        station_offset,
        station_values,
        tg_tile,
        target_cell.reshape(1, n_t),
        target_offset,
        cotangent,
        covariates,
    )
    recv = lax.all_to_all(send, axes, split_axis=0, concat_axis=0, tiled=True)

    north = lax.ppermute(covariates[:, 60:64, :], "lat", ring("lat", 1))
    south = lax.ppermute(covariates[:, 0:4, :], "lat", ring("lat", -1))
    west = lax.ppermute(to_east, "lon", ring("lon", 1))
    east = lax.ppermute(to_west, "lon", ring("lon", -1))

    sel = jnp.asarray(selection(), BF16)
    perm = jnp.asarray(permutation(), BF16)
    grads = call(
        main_kernel,
        shape(TILES, 1, 1792),
        scratch=[
            pltpu.VMEM((8, 128, 128), F32),
            pltpu.VMEM((5, 80, 256), F32),
            pltpu.VMEM((2, 80, 256), F32),
            pltpu.VMEM((256, 2048), BF16),
            pltpu.VMEM((400, 3072), BF16),
            pltpu.VMEM((144, 3072), BF16),
            pltpu.VMEM((2, 400, 128), F32),
            pltpu.VMEM((2, 80, 256), F32),
            pltpu.VMEM((4, 80, 128), F32),
            pltpu.VMEM((2, 160, 128), F32),
            pltpu.VMEM((2, 32, 256), F32),
            pltpu.VMEM((4, 32, 128), F32),
            pltpu.VMEM((9, 144, 512), F32),
            pltpu.VMEM((8, 72, 256), F32),
            pltpu.VMEM((9, 144, 128), BF16),
            pltpu.VMEM((7, 20, 144, 256), BF16),
            pltpu.VMEM((5, 18, 128, 256), BF16),
            pltpu.VMEM((5, 18, 128, 256), BF16),
            pltpu.VMEM((16, 128, 640), BF16),
            pltpu.VMEM((16, 128, 256), BF16),
            pltpu.VMEM((128, 128), F32),
            pltpu.VMEM((256, 2048), BF16),
            pltpu.VMEM((128, 128), F32),
            pltpu.VMEM((128, 128), F32),
            pltpu.VMEM((5, 512, 256), BF16),
            pltpu.VMEM((5, 512, 256), BF16),
            pltpu.VMEM((5, 512, 256), BF16),
            pltpu.VMEM((128, 512), BF16),
            pltpu.VMEM((128, 512), BF16),
            pltpu.VMEM((32, 256), BF16),
            pltpu.VMEM((1664, 128), F32),
        ],
        limit=52,
    )(recv, covariates, north, south, west, east, first_kernel, second_kernel, lift_weight, out_weight.T, sel)
    got = lax.all_to_all(grads, axes, split_axis=0, concat_axis=0, tiled=True)
    back, predictions = call(
        sum_kernel,
        (shape(TILES, 16, 128, dtype=BF16), shape(2, n_t)),
        limit=24,
    )(got, perm, tg_tile, tg_rank)
    summed = lax.all_to_all(back, axes, split_axis=0, concat_axis=0, tiled=True)
    grad_first, grad_second, grad_lift, grad_out = call(
        final_kernel,
        (shape(64, 1600), shape(64, 1600), shape(13, 64), shape(2, 64)),
        scratch=[pltpu.VMEM((TILES, 16, 128), F32)],
        limit=24,
    )(summed)
    return predictions, grad_lift, grad_first, grad_second, grad_out.T


def solution(mesh):
    placed = (
        P(("lat", "lon"), None),
        P(("lat", "lon")),
        P(None, ("lat", "lon")),
        P(None, ("lat", "lon")),
        P(None, "lat", "lon"),
        P(("lat", "lon"), None),
        P(("lat", "lon")),
        P(None, ("lat", "lon")),
        P(),
        P(),
        P(),
        P(),
        P(None, ("lat", "lon")),
    )
    return jax.shard_map(
        shards,
        mesh=mesh,
        in_specs=placed,
        out_specs=(P(None, ("lat", "lon")), P(), P(), P(), P()),
        check_vma=False,
    )
```

profile of v0, /device:TPU:1, one launch (start us, length us, event | category | flops | bytes accessed | tf_op | source)
XLA Modules:
  0.0 111.9 jit_solution(8420469619381014973)
XLA Ops:
  0.6 4.8 %shard_map.182 = (f32[128,8,128]{2,1,0:T(8,128)}, f32[16,256]{1,0:T(8,128)}, bf16[64,128]{1,0:T(8,128)(2,1)}, bf16[64,128]{1,0:T(8,128)(2,1)}) custom-call(s32[1,512]{1,0:T(1,128)} %bitcast.9, s32[1,512]{1,0:T(1,128)} %bitcast.10, f32[2,512]{1,0:T(2,128)} %st_off.1, f32[4,512]{1,0:T(4,128)} %st_val.1, s32[1,256]{1,0:T(1,128)} %bitcast.6, s32[1,256]{1,0:T(1,128)} %bitcast.11, ...), custom_call_target="tpu_custom_call" | custom-call | tf_op jit(solution)/shard_map/pallas_call | solution.py:902
  5.4 0.0 copy-start.10
  5.4 0.0 copy-start.9
  5.4 0.0 copy-start
  5.4 0.0 copy-start.1
  5.4 0.0 copy-start.2
  5.5 0.0 copy-start.3
  5.5 11.5 %all-to-all-start = ((f32[128,8,128]{2,1,0:T(8,128)}), f32[128,8,128]{2,1,0:T(8,128)S(1)}, u32[]{:S(2)}, u32[]{:S(2)}) async-start(f32[128,8,128]{2,1,0:T(8,128)} %get-tuple-element.15), calls=%async_computation | async-start | bytes 1048576 | tf_op jit(solution)/shard_map/all_to_all | solution.py:921
  17.0 0.0 copy-done.10
  17.0 1.7 %collective-permute-start.2 = (bf16[64,128]{1,0:T(8,128)(2,1)S(1)}, bf16[64,128]{1,0:T(8,128)(2,1)S(1)}, u32[]{:S(2)}, u32[]{:S(2)}) collective-permute-start(bf16[64,128]{1,0:T(8,128)(2,1)S(1)} %copy-done.10), channel_id=1, source_target_pairs={{0,1},{1,2},{2,3},{3,4},{4,5},{5,6},{6,7},{7,8},{8,9},{9,10},{10,1... | collective-permute-start | bytes 49160 | tf_op jit(solution)/shard_map/ppermute | solution.py:925
  18.7 0.0 copy-done.9
  18.7 0.0 collective-permute-start.3
  18.7 0.0 copy-done
  18.7 0.0 copy-start.6
  18.7 4.7 %collective-permute-start.1 = (bf16[8,4,128]{2,1,0:T(4,128)(2,1)S(1)}, bf16[8,4,128]{2,1,0:T(4,128)(2,1)S(1)}, u32[]{:S(2)}, u32[]{:S(2)}) collective-permute-start(bf16[8,4,128]{2,1,0:T(4,128)(2,1)S(1)} %get-tuple-element.25), channel_id=1, source_target_pairs={{0,112},{16,0},{32,16},{48,32},{64,48},{80,64},{96,80},{112,96},{1... | collective-permute-start | bytes 24584 | tf_op jit(solution)/shard_map/ppermute | solution.py:924
  23.4 0.0 copy-start.8
  23.4 0.0 collective-permute-start
  23.4 0.8 collective-permute-done.1.south
  24.3 5.6 %collective-permute-done.north = bf16[8,4,128]{2,1,0:T(4,128)(2,1)S(1)} collective-permute-done((bf16[8,4,128]{2,1,0:T(4,128)(2,1)S(1)}, bf16[8,4,128]{2,1,0:T(4,128)(2,1)S(1)}, u32[]{:S(2)}, u32[]{:S(2)}) %collective-permute-start) | collective-permute-done | bytes 8224 | tf_op jit(solution)/shard_map/ppermute | solution.py:923
  29.8 0.0 collective-permute-done.2.west
  29.8 0.0 collective-permute-done.3.east
  29.8 0.7 all-to-all-done.recv
  30.6 0.0 copy-done.1
  30.6 0.0 copy-done.2
  30.6 0.0 copy-done.3
  30.6 0.0 copy-done.6
  30.6 0.0 copy-done.8
  30.6 33.5 %shard_map.183 = f32[128,1,1792]{2,1,0:T(1,128)} custom-call(f32[128,8,128]{2,1,0:T(8,128)S(1)} %all-to-all-done.recv, bf16[8,64,128]{2,1,0:T(8,128)(2,1)S(1)} %copy-done, bf16[8,4,128]{2,1,0:T(4,128)(2,1)S(1)} %collective-permute-done.north, bf16[8,4,128]{2,1,0:T(4,128)(2,1)S(1)} %collective-permute-done.1.south, ...), custom_call_target="tpu_custom_call" | custom-call | tf_op jit(solution)/shard_map/pallas_call | solution.py:930
  64.1 0.0 copy-start.4
  64.1 0.0 copy-start.5
  64.1 25.6 %all_to_all.15.recv = f32[128,1,1792]{2,1,0:T(1,128)S(1)} all-to-all(f32[128,1,1792]{2,1,0:T(1,128)} %shard_map.183), channel_id=1, replica_groups=mesh['lat'=8,'lon'=16] {'lat','lon'}, dimensions={0} | all-to-all | bytes 1835008 | tf_op jit(solution)/shard_map/all_to_all | solution.py:968
  89.7 0.0 copy-start.7
  89.7 0.0 copy-done.4
  89.7 0.0 copy-done.5
  89.7 0.7 copy-done.7
  90.4 1.7 %shard_map.184 = (bf16[128,16,128]{2,1,0:T(8,128)(2,1)S(1)}, f32[2,256]{1,0:T(2,128)}) custom-call(f32[128,1,1792]{2,1,0:T(1,128)S(1)} %all_to_all.15.recv, bf16[4,16,896]{2,1,0:T(8,128)(2,1)S(1)} %copy-done.4, s32[1,256]{1,0:T(1,128)S(1)} %bitcast.7, f32[16,256]{1,0:T(8,128)S(1)} %copy-done.5), custom_call_target="tpu_custom_call" | custom-call | tf_op jit(solution)/shard_map/pallas_call | solution.py:969
  92.1 18.2 %all_to_all.16.recv = bf16[128,16,128]{2,1,0:T(8,128)(2,1)S(1)} all-to-all(bf16[128,16,128]{2,1,0:T(8,128)(2,1)S(1)} %get-tuple-element.20), channel_id=1, replica_groups=mesh['lat'=8,'lon'=16] {'lat','lon'}, dimensions={0} | all-to-all | bytes 1048576 | tf_op jit(solution)/shard_map/all_to_all | solution.py:974
  110.4 1.5 %shard_map.185 = (f32[64,1600]{1,0:T(8,128)}, f32[64,1600]{1,0:T(8,128)}, f32[13,64]{1,0:T(8,128)}, f32[2,64]{1,0:T(2,128)}) custom-call(bf16[128,16,128]{2,1,0:T(8,128)(2,1)S(1)} %all_to_all.16.recv), custom_call_target="tpu_custom_call" | custom-call | tf_op jit(solution)/shard_map/pallas_call | solution.py:975
  (1 shorter events, 0.0 us)
Async XLA Ops:
  5.4 11.6 %copy-start.10 = (bf16[64,128]{1,0:T(8,128)(2,1)S(1)}, bf16[64,128]{1,0:T(8,128)(2,1)}, u32[]{:S(2)}) copy-start(bf16[64,128]{1,0:T(8,128)(2,1)} %get-tuple-element.16) | copy-start | bytes 49156
  5.4 13.3 %copy-start.9 = (bf16[64,128]{1,0:T(8,128)(2,1)S(1)}, bf16[64,128]{1,0:T(8,128)(2,1)}, u32[]{:S(2)}) copy-start(bf16[64,128]{1,0:T(8,128)(2,1)} %get-tuple-element.17) | copy-start | bytes 49156
  5.4 13.3 %copy-start = (bf16[8,64,128]{2,1,0:T(8,128)(2,1)S(1)}, bf16[8,64,128]{2,1,0:T(8,128)(2,1)}, u32[]{:S(2)}) copy-start(bf16[8,64,128]{2,1,0:T(8,128)(2,1)} %cov.3) | copy-start | bytes 393220
  5.4 25.1 %copy-start.1 = (bf16[64,1600]{1,0:T(8,128)(2,1)S(1)}, bf16[64,1600]{1,0:T(8,128)(2,1)}, u32[]{:S(2)}) copy-start(bf16[64,1600]{1,0:T(8,128)(2,1)} %k1.1) | copy-start | bytes 614404
  5.4 25.1 %copy-start.2 = (bf16[64,1600]{1,0:T(8,128)(2,1)S(1)}, bf16[64,1600]{1,0:T(8,128)(2,1)}, u32[]{:S(2)}) copy-start(bf16[64,1600]{1,0:T(8,128)(2,1)} %k2.1) | copy-start | bytes 614404
  5.5 25.1 %copy-start.3 = (bf16[256,256]{1,0:T(8,128)(2,1)S(1)}, bf16[256,256]{1,0:T(8,128)(2,1)}, u32[]{:S(2)}) copy-start(bf16[256,256]{1,0:T(8,128)(2,1)} %constant.4.clone.sel) | copy-start | bytes 393220
  5.5 25.1 %all-to-all-start = ((f32[128,8,128]{2,1,0:T(8,128)}), f32[128,8,128]{2,1,0:T(8,128)S(1)}, u32[]{:S(2)}, u32[]{:S(2)}) async-start(f32[128,8,128]{2,1,0:T(8,128)} %get-tuple-element.15), calls=%async_computation | async-start | bytes 1048576 | tf_op jit(solution)/shard_map/all_to_all | solution.py:921
  17.0 12.8 %collective-permute-start.2 = (bf16[64,128]{1,0:T(8,128)(2,1)S(1)}, bf16[64,128]{1,0:T(8,128)(2,1)S(1)}, u32[]{:S(2)}, u32[]{:S(2)}) collective-permute-start(bf16[64,128]{1,0:T(8,128)(2,1)S(1)} %copy-done.10), channel_id=1, source_target_pairs={{0,1},{1,2},{2,3},{3,4},{4,5},{5,6},{6,7},{7,8},{8,9},{9,10},{10,1... | collective-permute-start | bytes 49160 | tf_op jit(solution)/shard_map/ppermute | solution.py:925
  18.7 11.1 %collective-permute-start.3 = (bf16[64,128]{1,0:T(8,128)(2,1)S(1)}, bf16[64,128]{1,0:T(8,128)(2,1)S(1)}, u32[]{:S(2)}, u32[]{:S(2)}) collective-permute-start(bf16[64,128]{1,0:T(8,128)(2,1)S(1)} %copy-done.9), channel_id=1, source_target_pairs={{0,15},{1,0},{2,1},{3,2},{4,3},{5,4},{6,5},{7,6},{8,7},{9,8},{10,9... | collective-permute-start | bytes 49160 | tf_op jit(solution)/shard_map/ppermute | solution.py:926
  18.7 11.8 %copy-start.6 = (bf16[13,64]{1,0:T(8,128)(2,1)S(1)}, bf16[13,64]{1,0:T(8,128)(2,1)}, u32[]{:S(2)}) copy-start(bf16[13,64]{1,0:T(8,128)(2,1)} %lift_w.1) | copy-start | bytes 4996
  18.7 5.5 %collective-permute-start.1 = (bf16[8,4,128]{2,1,0:T(4,128)(2,1)S(1)}, bf16[8,4,128]{2,1,0:T(4,128)(2,1)S(1)}, u32[]{:S(2)}, u32[]{:S(2)}) collective-permute-start(bf16[8,4,128]{2,1,0:T(4,128)(2,1)S(1)} %get-tuple-element.25), channel_id=1, source_target_pairs={{0,112},{16,0},{32,16},{48,32},{64,48},{80,64},{96,80},{112,96},{1... | collective-permute-start | bytes 24584 | tf_op jit(solution)/shard_map/ppermute | solution.py:924
  23.4 7.2 %copy-start.8 = (f32[64,2]{0,1:T(2,128)S(1)}, f32[64,2]{0,1:T(2,128)}, u32[]{:S(2)}) copy-start(f32[64,2]{0,1:T(2,128)} %param.26) | copy-start | bytes 1540
  23.4 6.4 %collective-permute-start = (bf16[8,4,128]{2,1,0:T(4,128)(2,1)S(1)}, bf16[8,4,128]{2,1,0:T(4,128)(2,1)S(1)}, u32[]{:S(2)}, u32[]{:S(2)}) collective-permute-start(bf16[8,4,128]{2,1,0:T(4,128)(2,1)S(1)} %get-tuple-element.26), channel_id=1, source_target_pairs={{0,16},{16,32},{32,48},{48,64},{64,80},{80,96},{96,112},{112,0},{1... | collective-permute-start | bytes 24584 | tf_op jit(solution)/shard_map/ppermute | solution.py:923
  64.1 25.6 %copy-start.4 = (bf16[4,16,896]{2,1,0:T(8,128)(2,1)S(1)}, bf16[4,16,896]{2,1,0:T(8,128)(2,1)}, u32[]{:S(2)}) copy-start(bf16[4,16,896]{2,1,0:T(8,128)(2,1)} %constant.5.clone.perm) | copy-start | bytes 344068
  64.1 25.6 %copy-start.5 = (f32[16,256]{1,0:T(8,128)S(1)}, f32[16,256]{1,0:T(8,128)}, u32[]{:S(2)}) copy-start(f32[16,256]{1,0:T(8,128)} %get-tuple-element.18.tg_rank) | copy-start | bytes 49156
  89.7 0.7 copy-start.7
where the time goes:
time: 112 us
  blocking collectives  43.9 us (39%)
  Pallas kernels  41.5 us (37%)
  starting transfers between devices  17.9 us (16%)
  waiting for transfers between devices  7.14 us (6%)
    pallas_call x1, Pallas kernels, shards(): call(main_kernel, shape(TILES, 1, 1792), scratch=[pltpu.VMEM((8, 128, 128...  33.5 us
    all_to_all x1, blocking collectives, shards(): got = lax.all_to_all(grads, axes, split_axis=0, concat_axis=0, tiled=True)  25.6 us
    all_to_all x1, blocking collectives, shards(): summed = lax.all_to_all(back, axes, split_axis=0, concat_axis=0, tiled=True)  18.2 us
    all_to_all x1, starting transfers between devices, shards(): recv = lax.all_to_all(send, axes, split_axis=0, concat_axis=0, tiled=True)  11.5 us
    ppermute x1, waiting for transfers between devices, shards(): north = lax.ppermute(covariates[:, 60:64, :], 'lat', ring('lat', 1))  5.56 us
    pallas_call x1, Pallas kernels, shards(): call(pack_kernel, (shape(TILES, 8, 128), shape(16, n_t), shape(64, 128, d...  4.78 us
    ppermute x1, starting transfers between devices, shards(): south = lax.ppermute(covariates[:, 0:4, :], 'lat', ring('lat', -1))  4.67 us
  transfers between devices with their start and end apart: 5, of which 3 were waited for; matrix products, arithmetic and copies ran while one was open for 0% of the time, Pallas kernels for 0%

commit v1 on v0

--- a/solution.py
+++ b/solution.py
@@ -654,13 +654,13 @@
         own = x1[4, pl.ds(4 * c + 2, 4), 0:128, :].reshape(512, 256)
         latent = (own.astype(F32) + value).astype(BF16)
         lat[pl.ds(4 * c, 4)] = latent.reshape(4, 128, 256)
-        outs = dot(wdec[...], latent, NT)
-        outs = outs[0:8] + outs[8:16] + outs[16:24]
-        for i in range(4):
-            lmat[pl.ds(pl.multiple_of(32 * c + 8 * i, 8), 8), :] = outs[:, 128 * i : 128 * i + 128]
         return carry
 
     lax.fori_loop(0, 4, latent_step, 0)
+    outs = dot(wdec[...], lat[...].reshape(2048, 256), NT)
+    outs = outs[0:8] + outs[8:16] + outs[16:24]
+    for i in range(16):
+        lmat[8 * i : 8 * i + 8, :] = outs[:, 128 * i : 128 * i + 128]
 
     grad_out = jnp.zeros((48, 512), F32)
     for m in range(8):

time: 112 us -> 112 us (level)
  no operation moved by 1% of the time
where the time goes in v1:
time: 112 us; the launch traced here: 111 us
  blocking collectives  43.1 us (38%)
  Pallas kernels  41.8 us (37%)
  starting transfers between devices  17.9 us (16%)
  waiting for transfers between devices  7.14 us (6%)
    pallas_call x1, Pallas kernels, shards(): call(main_kernel, shape(TILES, 1, 1792), scratch=[pltpu.VMEM((8, 128, 128...  33.8 us
    all_to_all x1, blocking collectives, shards(): got = lax.all_to_all(grads, axes, split_axis=0, concat_axis=0, tiled=True)  24.9 us
    all_to_all x1, blocking collectives, shards(): summed = lax.all_to_all(back, axes, split_axis=0, concat_axis=0, tiled=True)  18.2 us
    all_to_all x1, starting transfers between devices, shards(): recv = lax.all_to_all(send, axes, split_axis=0, concat_axis=0, tiled=True)  11.5 us
    ppermute x1, waiting for transfers between devices, shards(): north = lax.ppermute(covariates[:, 60:64, :], 'lat', ring('lat', 1))  5.56 us
    pallas_call x1, Pallas kernels, shards(): call(pack_kernel, (shape(TILES, 8, 128), shape(16, n_t), shape(64, 128, d...  4.78 us
    ppermute x1, starting transfers between devices, shards(): south = lax.ppermute(covariates[:, 0:4, :], 'lat', ring('lat', -1))  4.67 us
  transfers between devices with their start and end apart: 5, of which 3 were waited for; matrix products, arithmetic and copies ran while one was open for 0% of the time, Pallas kernels for 0%

profile of v1, /device:TPU:1, one launch (start us, length us, event | category | flops | bytes accessed | tf_op | source)
XLA Modules:
  0.0 111.5 jit_solution(10724007536698583508)
XLA Ops:
  0.6 4.8 %shard_map.182 = (f32[128,8,128]{2,1,0:T(8,128)}, f32[16,256]{1,0:T(8,128)}, bf16[64,128]{1,0:T(8,128)(2,1)}, bf16[64,128]{1,0:T(8,128)(2,1)}) custom-call(s32[1,512]{1,0:T(1,128)} %bitcast.9, s32[1,512]{1,0:T(1,128)} %bitcast.10, f32[2,512]{1,0:T(2,128)} %st_off.1, f32[4,512]{1,0:T(4,128)} %st_val.1, s32[1,256]{1,0:T(1,128)} %bitcast.6, s32[1,256]{1,0:T(1,128)} %bitcast.11, ...), custom_call_target="tpu_custom_call" | custom-call | tf_op jit(solution)/shard_map/pallas_call | solution.py:902
  5.4 0.0 copy-start.10
  5.4 0.0 copy-start.9
  5.4 0.0 copy-start
  5.4 0.0 copy-start.1
  5.4 0.0 copy-start.2
  5.5 0.0 copy-start.3
  5.5 11.5 %all-to-all-start = ((f32[128,8,128]{2,1,0:T(8,128)}), f32[128,8,128]{2,1,0:T(8,128)S(1)}, u32[]{:S(2)}, u32[]{:S(2)}) async-start(f32[128,8,128]{2,1,0:T(8,128)} %get-tuple-element.15), calls=%async_computation | async-start | bytes 1048576 | tf_op jit(solution)/shard_map/all_to_all | solution.py:921
  17.0 0.0 copy-done.10
  17.0 1.7 %collective-permute-start.2 = (bf16[64,128]{1,0:T(8,128)(2,1)S(1)}, bf16[64,128]{1,0:T(8,128)(2,1)S(1)}, u32[]{:S(2)}, u32[]{:S(2)}) collective-permute-start(bf16[64,128]{1,0:T(8,128)(2,1)S(1)} %copy-done.10), channel_id=1, source_target_pairs={{0,1},{1,2},{2,3},{3,4},{4,5},{5,6},{6,7},{7,8},{8,9},{9,10},{10,1... | collective-permute-start | bytes 49160 | tf_op jit(solution)/shard_map/ppermute | solution.py:925
  18.7 0.0 copy-done.9
  18.7 0.0 collective-permute-start.3
  18.7 0.0 copy-done
  18.7 0.0 copy-start.6
  18.7 4.7 %collective-permute-start.1 = (bf16[8,4,128]{2,1,0:T(4,128)(2,1)S(1)}, bf16[8,4,128]{2,1,0:T(4,128)(2,1)S(1)}, u32[]{:S(2)}, u32[]{:S(2)}) collective-permute-start(bf16[8,4,128]{2,1,0:T(4,128)(2,1)S(1)} %get-tuple-element.25), channel_id=1, source_target_pairs={{0,112},{16,0},{32,16},{48,32},{64,48},{80,64},{96,80},{112,96},{1... | collective-permute-start | bytes 24584 | tf_op jit(solution)/shard_map/ppermute | solution.py:924
  23.4 0.0 copy-start.8
  23.4 0.0 collective-permute-start
  23.4 0.8 collective-permute-done.1.south
  24.3 5.6 %collective-permute-done.north = bf16[8,4,128]{2,1,0:T(4,128)(2,1)S(1)} collective-permute-done((bf16[8,4,128]{2,1,0:T(4,128)(2,1)S(1)}, bf16[8,4,128]{2,1,0:T(4,128)(2,1)S(1)}, u32[]{:S(2)}, u32[]{:S(2)}) %collective-permute-start) | collective-permute-done | bytes 8224 | tf_op jit(solution)/shard_map/ppermute | solution.py:923
  29.8 0.0 collective-permute-done.2.west
  29.8 0.0 collective-permute-done.3.east
  29.8 0.7 all-to-all-done.recv
  30.6 0.0 copy-done.1
  30.6 0.0 copy-done.2
  30.6 0.0 copy-done.3
  30.6 0.0 copy-done.6
  30.6 0.0 copy-done.8
  30.6 33.8 %shard_map.183 = f32[128,1,1792]{2,1,0:T(1,128)} custom-call(f32[128,8,128]{2,1,0:T(8,128)S(1)} %all-to-all-done.recv, bf16[8,64,128]{2,1,0:T(8,128)(2,1)S(1)} %copy-done, bf16[8,4,128]{2,1,0:T(4,128)(2,1)S(1)} %collective-permute-done.north, bf16[8,4,128]{2,1,0:T(4,128)(2,1)S(1)} %collective-permute-done.1.south, ...), custom_call_target="tpu_custom_call" | custom-call | tf_op jit(solution)/shard_map/pallas_call | solution.py:930
  64.4 0.0 copy-start.4
  64.4 0.0 copy-start.5
  64.4 24.9 %all_to_all.15.recv = f32[128,1,1792]{2,1,0:T(1,128)S(1)} all-to-all(f32[128,1,1792]{2,1,0:T(1,128)} %shard_map.183), channel_id=1, replica_groups=mesh['lat'=8,'lon'=16] {'lat','lon'}, dimensions={0} | all-to-all | bytes 1835008 | tf_op jit(solution)/shard_map/all_to_all | solution.py:968
  89.3 0.0 copy-start.7
  89.3 0.0 copy-done.4
  89.3 0.0 copy-done.5
  89.3 0.7 copy-done.7
  90.0 1.7 %shard_map.184 = (bf16[128,16,128]{2,1,0:T(8,128)(2,1)S(1)}, f32[2,256]{1,0:T(2,128)}) custom-call(f32[128,1,1792]{2,1,0:T(1,128)S(1)} %all_to_all.15.recv, bf16[4,16,896]{2,1,0:T(8,128)(2,1)S(1)} %copy-done.4, s32[1,256]{1,0:T(1,128)S(1)} %bitcast.7, f32[16,256]{1,0:T(8,128)S(1)} %copy-done.5), custom_call_target="tpu_custom_call" | custom-call | tf_op jit(solution)/shard_map/pallas_call | solution.py:969
  91.7 18.2 %all_to_all.16.recv = bf16[128,16,128]{2,1,0:T(8,128)(2,1)S(1)} all-to-all(bf16[128,16,128]{2,1,0:T(8,128)(2,1)S(1)} %get-tuple-element.20), channel_id=1, replica_groups=mesh['lat'=8,'lon'=16] {'lat','lon'}, dimensions={0} | all-to-all | bytes 1048576 | tf_op jit(solution)/shard_map/all_to_all | solution.py:974
  110.0 1.5 %shard_map.185 = (f32[64,1600]{1,0:T(8,128)}, f32[64,1600]{1,0:T(8,128)}, f32[13,64]{1,0:T(8,128)}, f32[2,64]{1,0:T(2,128)}) custom-call(bf16[128,16,128]{2,1,0:T(8,128)(2,1)S(1)} %all_to_all.16.recv), custom_call_target="tpu_custom_call" | custom-call | tf_op jit(solution)/shard_map/pallas_call | solution.py:975
  (1 shorter events, 0.0 us)
Async XLA Ops:
  5.4 11.6 %copy-start.10 = (bf16[64,128]{1,0:T(8,128)(2,1)S(1)}, bf16[64,128]{1,0:T(8,128)(2,1)}, u32[]{:S(2)}) copy-start(bf16[64,128]{1,0:T(8,128)(2,1)} %get-tuple-element.16) | copy-start | bytes 49156
  5.4 13.3 %copy-start.9 = (bf16[64,128]{1,0:T(8,128)(2,1)S(1)}, bf16[64,128]{1,0:T(8,128)(2,1)}, u32[]{:S(2)}) copy-start(bf16[64,128]{1,0:T(8,128)(2,1)} %get-tuple-element.17) | copy-start | bytes 49156
  5.4 13.3 %copy-start = (bf16[8,64,128]{2,1,0:T(8,128)(2,1)S(1)}, bf16[8,64,128]{2,1,0:T(8,128)(2,1)}, u32[]{:S(2)}) copy-start(bf16[8,64,128]{2,1,0:T(8,128)(2,1)} %cov.3) | copy-start | bytes 393220
  5.4 25.1 %copy-start.1 = (bf16[64,1600]{1,0:T(8,128)(2,1)S(1)}, bf16[64,1600]{1,0:T(8,128)(2,1)}, u32[]{:S(2)}) copy-start(bf16[64,1600]{1,0:T(8,128)(2,1)} %k1.1) | copy-start | bytes 614404
  5.4 25.1 %copy-start.2 = (bf16[64,1600]{1,0:T(8,128)(2,1)S(1)}, bf16[64,1600]{1,0:T(8,128)(2,1)}, u32[]{:S(2)}) copy-start(bf16[64,1600]{1,0:T(8,128)(2,1)} %k2.1) | copy-start | bytes 614404
  5.5 25.1 %copy-start.3 = (bf16[256,256]{1,0:T(8,128)(2,1)S(1)}, bf16[256,256]{1,0:T(8,128)(2,1)}, u32[]{:S(2)}) copy-start(bf16[256,256]{1,0:T(8,128)(2,1)} %constant.4.clone.sel) | copy-start | bytes 393220
  5.5 25.1 %all-to-all-start = ((f32[128,8,128]{2,1,0:T(8,128)}), f32[128,8,128]{2,1,0:T(8,128)S(1)}, u32[]{:S(2)}, u32[]{:S(2)}) async-start(f32[128,8,128]{2,1,0:T(8,128)} %get-tuple-element.15), calls=%async_computation | async-start | bytes 1048576 | tf_op jit(solution)/shard_map/all_to_all | solution.py:921
  17.0 12.8 %collective-permute-start.2 = (bf16[64,128]{1,0:T(8,128)(2,1)S(1)}, bf16[64,128]{1,0:T(8,128)(2,1)S(1)}, u32[]{:S(2)}, u32[]{:S(2)}) collective-permute-start(bf16[64,128]{1,0:T(8,128)(2,1)S(1)} %copy-done.10), channel_id=1, source_target_pairs={{0,1},{1,2},{2,3},{3,4},{4,5},{5,6},{6,7},{7,8},{8,9},{9,10},{10,1... | collective-permute-start | bytes 49160 | tf_op jit(solution)/shard_map/ppermute | solution.py:925
  18.7 11.1 %collective-permute-start.3 = (bf16[64,128]{1,0:T(8,128)(2,1)S(1)}, bf16[64,128]{1,0:T(8,128)(2,1)S(1)}, u32[]{:S(2)}, u32[]{:S(2)}) collective-permute-start(bf16[64,128]{1,0:T(8,128)(2,1)S(1)} %copy-done.9), channel_id=1, source_target_pairs={{0,15},{1,0},{2,1},{3,2},{4,3},{5,4},{6,5},{7,6},{8,7},{9,8},{10,9... | collective-permute-start | bytes 49160 | tf_op jit(solution)/shard_map/ppermute | solution.py:926
  18.7 11.8 %copy-start.6 = (bf16[13,64]{1,0:T(8,128)(2,1)S(1)}, bf16[13,64]{1,0:T(8,128)(2,1)}, u32[]{:S(2)}) copy-start(bf16[13,64]{1,0:T(8,128)(2,1)} %lift_w.1) | copy-start | bytes 4996
  18.7 5.5 %collective-permute-start.1 = (bf16[8,4,128]{2,1,0:T(4,128)(2,1)S(1)}, bf16[8,4,128]{2,1,0:T(4,128)(2,1)S(1)}, u32[]{:S(2)}, u32[]{:S(2)}) collective-permute-start(bf16[8,4,128]{2,1,0:T(4,128)(2,1)S(1)} %get-tuple-element.25), channel_id=1, source_target_pairs={{0,112},{16,0},{32,16},{48,32},{64,48},{80,64},{96,80},{112,96},{1... | collective-permute-start | bytes 24584 | tf_op jit(solution)/shard_map/ppermute | solution.py:924
  23.4 7.2 %copy-start.8 = (f32[64,2]{0,1:T(2,128)S(1)}, f32[64,2]{0,1:T(2,128)}, u32[]{:S(2)}) copy-start(f32[64,2]{0,1:T(2,128)} %param.26) | copy-start | bytes 1540
  23.4 6.4 %collective-permute-start = (bf16[8,4,128]{2,1,0:T(4,128)(2,1)S(1)}, bf16[8,4,128]{2,1,0:T(4,128)(2,1)S(1)}, u32[]{:S(2)}, u32[]{:S(2)}) collective-permute-start(bf16[8,4,128]{2,1,0:T(4,128)(2,1)S(1)} %get-tuple-element.26), channel_id=1, source_target_pairs={{0,16},{16,32},{32,48},{48,64},{64,80},{80,96},{96,112},{112,0},{1... | collective-permute-start | bytes 24584 | tf_op jit(solution)/shard_map/ppermute | solution.py:923
  64.4 24.9 %copy-start.4 = (bf16[4,16,896]{2,1,0:T(8,128)(2,1)S(1)}, bf16[4,16,896]{2,1,0:T(8,128)(2,1)}, u32[]{:S(2)}) copy-start(bf16[4,16,896]{2,1,0:T(8,128)(2,1)} %constant.5.clone.perm) | copy-start | bytes 344068
  64.4 24.9 %copy-start.5 = (f32[16,256]{1,0:T(8,128)S(1)}, f32[16,256]{1,0:T(8,128)}, u32[]{:S(2)}) copy-start(f32[16,256]{1,0:T(8,128)} %get-tuple-element.18.tg_rank) | copy-start | bytes 49156
  89.3 0.7 copy-start.7
